TPU v7x, 256 devices: a whole 4x4x8 slice. The times are simulated.
256 devices in a mesh: ctx: 32 (over z, y_hi, core), ch: 8 (over x, y_lo).
Axes of the slice: x: 4, y: 4 (y_hi: 2, y_lo: 2; y = y_hi * 2 + y_lo), z: 8, core: 2. Of those that a mesh axis runs over, the one named last changes fastest.
Arguments:
- query_proj: bfloat16 [4096, 8192], P('ctx', 'ch'), may hold values from -6 to 6
- key_proj: bfloat16 [4096, 8192], P('ctx', 'ch'), may hold values from -6 to 6
- value_proj: bfloat16 [4096, 8192], P('ctx', 'ch'), may hold values from -6 to 6
- pole_rate: float32 [16, 8192], P(None, 'ch'), may hold values from 1.4648438e-06 to 0.05
- residue: float32 [16, 8192], P(None, 'ch'), may hold values from -2 to 2
- direct_gain: float32 [8192], P('ch'), may hold values from -4 to 4
- out_weight: bfloat16 [8192, 8192], P('ch', 'ctx'), may hold values from -0.125 to 0.125
Outputs:
- layer_out: bfloat16 [4096, 8192], P('ctx', 'ch')
All inputs are finite; a program needn't handle non-finite values.
Results may differ from a plain program's by a relative error of at most 0.017.
Values may be sent and summed in bfloat16 or wider, within the bound.
A program may use at most 64 MiB of HBM per device.

v0:
```python
import jax
import jax.numpy as jnp
from jax import lax
from jax.sharding import PartitionSpec as P


def entering(part, axis, combine, identity):
    place = lax.axis_index(axis)
    gathered = jax.tree.map(lambda a: lax.all_gather(a, axis), part)
    state = jax.tree.map(lambda a, e: jnp.zeros_like(a) + jnp.asarray(e, a.dtype), part, identity)

    def one(lap, state):
        return combine(
            state, jax.tree.map(lambda a: lax.dynamic_index_in_dim(a, lap, 0, False), gathered)
        )

    return lax.fori_loop(0, place, one, state)


def link_pairs(earlier, later):
    return (earlier[0] * later[0], later[0] * earlier[1] + later[1])


def local_terms(stream, rate, coef, direct):
    block_len = 16
    length, width = stream.shape
    count = length // block_len
    grid = stream.reshape(count, block_len, width)
    steps = jnp.arange(block_len, dtype=jnp.float32)
    lag_decay = jnp.exp(-rate[:, None, :] * steps[None, :, None])
    taps = jnp.sum(coef[:, None, :] * lag_decay, axis=0)
    inner = direct[None, None, :] * grid
    for lag in range(block_len):
        moved = jnp.pad(grid, ((0, 0), (lag, 0), (0, 0)))[:, :block_len]
        inner = inner + taps[lag][None, None, :] * moved
    weigh_in = jnp.exp(-rate[:, None, :] * (block_len - 1.0 - steps)[None, :, None])
    summary = jnp.zeros((rate.shape[0], count, width), jnp.float32)
    for place in range(block_len):
        summary = summary + weigh_in[:, place][:, None, :] * grid[:, place][None, :, :]
    step_decay = jnp.broadcast_to(jnp.exp(-rate * block_len)[:, None, :], summary.shape)
    _, ending = lax.associative_scan(link_pairs, (step_decay, summary), axis=1)
    before = jnp.concatenate([jnp.zeros_like(ending[:, :1]), ending[:, :-1]], axis=1)
    return (inner, before, ending[:, -1])


def add_entry(inner, before, rate, coef, entry):
    count, block_len, width = inner.shape
    steps = jnp.arange(block_len, dtype=jnp.float32)
    starts = jnp.arange(count, dtype=jnp.float32) * block_len
    before = before + jnp.exp(-rate[:, None, :] * starts[None, :, None]) * entry[:, None, :]
    weigh_out = coef[:, None, :] * jnp.exp(-rate[:, None, :] * (steps + 1.0)[None, :, None])
    outer = jnp.zeros((count, block_len, width), jnp.float32)
    for pole in range(rate.shape[0]):
        outer = outer + weigh_out[pole][None, :, :] * before[pole][:, None, :]
    return (inner + outer).reshape(count * block_len, width)


def shards(query_proj, key_proj, value_proj, pole_rate, residue, direct_gain, out_weight):
    coef = residue * jnp.sqrt(-jnp.expm1(-2.0 * pole_rate))
    stream = key_proj.astype(jnp.float32) * value_proj.astype(jnp.float32)
    length = stream.shape[0]
    inner, before, ending = local_terms(stream, pole_rate, coef, direct_gain)
    block_decay = jnp.exp(-pole_rate * length)
    identity = (jnp.ones_like(block_decay), jnp.zeros_like(ending))
    _, entry = entering((block_decay, ending), "ctx", link_pairs, identity)
    conv = add_entry(inner, before, pole_rate, coef, entry)
    hidden = (query_proj.astype(jnp.float32) * conv).astype(jnp.bfloat16)
    terms = jnp.dot(
        hidden,
        lax.all_gather(out_weight, "ctx", axis=1, tiled=True),
        preferred_element_type=jnp.float32,
    )
    mixed = lax.psum_scatter(terms.astype(jnp.bfloat16), "ch", scatter_dimension=1, tiled=True)
    return mixed


def solution(mesh):
    return jax.shard_map(
        shards,
        mesh=mesh,
        in_specs=(
            P("ctx", "ch"),
            P("ctx", "ch"),
            P("ctx", "ch"),
            P(None, "ch"),
            P(None, "ch"),
            P("ch"),
            P("ch", "ctx"),
        ),
        out_specs=P("ctx", "ch"),
        check_vma=False,
    )
```

profile of v0, /device:TPU:4, one launch (start us, length us, event | category | flops | bytes accessed | tf_op | source)
XLA Modules:
  0.0 392.7 jit_solution(2932188920302415106)
XLA Ops:
  6.5 1.1 convert_multiply_fusion
  7.7 0.5 fusion.39
  8.2 0.7 multiply_exponential_fusion.1
  8.8 1.3 exponential_multiply_fusion
  10.2 0.1 slice_bitcast_fusion.15
  10.5 0.6 multiply_add_fusion.1
  11.4 0.1 pad.230
  11.5 0.6 slice.700
  12.2 0.7 all-gather.8.cloned.1.call-update
  12.9 0.7 all-gather.6.cloned.1.call-update
  13.6 0.6 slice.511
  14.3 0.1 pad.100
  14.4 0.9 pad_maximum_fusion
  15.3 0.1 pad.99
  15.4 0.9 fusion.37
  16.8 78.4 %all-gather.10.cloned.1.call-done = f32[512,1,1024]{2,0,1:T(8,128)} async-done(((f32[16,1,1024]{2,0,1:T(8,128)}), f32[512,1,1024]{2,0,1:T(8,128)}) %all-gather.10.cloned.1.call-update) | async-done | bytes 2097168 | tf_op jit(solution)/shard_map/all_gather | solution.py:9
  95.1 79.4 %all-gather.8.cloned.1.call-done = f32[512,1024]{1,0:T(8,128)} async-done(((f32[16,1024]{1,0:T(8,128)}), f32[512,1024]{1,0:T(8,128)}) %all-gather.8.cloned.1.call-update) | async-done | bytes 2097168 | tf_op jit(solution)/shard_map/all_gather | solution.py:9
  174.5 0.2 multiply_add_fusion
  174.7 0.5 fusion.38
  175.4 1.8 fusion.16
  177.2 0.1 fusion.31
  177.3 149.1 %all-gather.6.cloned.1.call-done = bf16[1024,8192]{1,0:T(8,128)(2,1)} async-done(((bf16[1024,256]{1,0:T(8,128)(2,1)}), bf16[1024,8192]{1,0:T(8,128)(2,1)}) %all-gather.6.cloned.1.call-update) | async-done | bytes 16777232 | tf_op jit(solution)/shard_map/all_gather | solution.py:70
  326.4 9.5 %convolution_convert_fusion = bf16[128,8192]{1,0:T(8,128)(2,1)} fusion(bf16[128,1024]{1,0:T(8,128)(2,1)S(1)} %fusion.31, bf16[1024,8192]{1,0:T(8,128)(2,1)} %all-gather.6.cloned.1.call-done), kind=kOutput, calls=%fused_computation.2 | convolution fusion | flops 2148532224 | bytes 19136512 | tf_op jit(solution)/shard_map/dot_general | solution.py:68
  335.9 50.3 %reduce-scatter.2.cloned.1.call-done = bf16[128,1024]{1,0:T(8,128)(2,1)} async-done(((bf16[128,8192]{1,0:T(8,128)(2,1)}), bf16[128,1024]{1,0:T(8,128)(2,1)}) %reduce-scatter.2.cloned.1.call-update) | async-done | bytes 262160 | tf_op jit(solution)/shard_map/reduce_scatter | solution.py:73
  (73 shorter events, 1.1 us)
Async XLA Ops:
  6.5 1.6 copy-start
  6.5 1.6 copy-start.3
  6.5 88.6 %all-gather.10.cloned.1.call-start = ((), (), s32[]{:S(2)}) async-start(), calls=%async_computation.4 | async-start | bytes 2162688 | tf_op jit(solution)/shard_map/all_gather | solution.py:9
  12.1 162.4 %all-gather.8.cloned.1.call-start = ((), (), s32[]{:S(2)}) async-start(), calls=%async_computation.3 | async-start | bytes 2162688 | tf_op jit(solution)/shard_map/all_gather | solution.py:9
  12.9 313.5 %all-gather.6.cloned.1.call-start = ((), (), s32[]{:S(2)}) async-start(), calls=%async_computation.1 | async-start | bytes 17301504 | tf_op jit(solution)/shard_map/all_gather | solution.py:70
  13.6 372.6 %reduce-scatter.2.cloned.1.call-start = ((), (), s32[]{:S(2)}) async-start(), calls=%async_computation.2 | async-start | bytes 2359296 | tf_op jit(solution)/shard_map/reduce_scatter | solution.py:73
  15.3 1.3 copy-start.1
  15.3 1.3 copy-start.4
  175.1 2.0 copy-start.2
Sparse Core Ops, SparseCore 0:
  12.2 82.8 all-gather.9
  97.9 76.5 all-gather.7
  177.1 149.2 all-gather.5
  336.0 50.1 reduce-scatter.1
where the time goes:
time: 395 us; the launch traced here: 393 us
  waiting for transfers between devices  359 us (91%)
  between operations  13.7 us (3%)
  matrix products  9.47 us (2%)
  other arithmetic  6.89 us (2%)
  local copies, waits for them, and re-layouts  4 us (1%)
    all_gather x2, waiting for transfers between devices, entering(): gathered = jax.tree.map(lambda a: lax.all_gather(a, axis), part)  158 us
    all_gather x1, waiting for transfers between devices, shards(): lax.all_gather(out_weight, 'ctx', axis=1, tiled=True)  149 us
    reduce_scatter x1, waiting for transfers between devices, shards(): lax.psum_scatter(terms.astype(jnp.bfloat16), 'ch', scatter_dimension=1, t...  50.3 us
    dot_general x1, matrix products, shards(): jnp.dot(hidden, lax.all_gather(out_weight, 'ctx', axis=1, tiled=True), pr...  9.47 us
  transfers between devices with their start and end apart: 4, of which 4 were waited for; matrix products, arithmetic and copies ran while one was open for 1% of the time, Pallas kernels for 0%

commit v1 on v0

v1 whole, which is shorter than its diff:
```python
import jax
import jax.numpy as jnp
from jax import lax
from jax.experimental import pallas as pl
from jax.experimental.pallas import tpu as pltpu
from jax.sharding import PartitionSpec as P

MESH = pl.DeviceIdType.MESH
BF = jnp.bfloat16
F32 = jnp.float32
POLES = 16
ROWS = 128
WIDTH = 1024
CHUNKS = 8
STEPS = 16
CTX = 32
OFFSETS = (0, -1, 1, -2, 2, -3, 3, 4)
ROUNDS = ((0,), (1, 2), (3, 4), (5, 6), (7,))


def one_minus_exp(x):
    series = 1.0 - x / 8.0
    for k in (7.0, 6.0, 5.0, 4.0, 3.0, 2.0):
        series = 1.0 - x / k * series
    return jnp.where(x < 0.125, x * series, 1.0 - jnp.exp(-x))


def spread(rows):
    return jnp.broadcast_to(rows[:, None, :], (POLES, CHUNKS, 128))


def kernel(
    q_hbm, k_hbm, v_hbm, rate_hbm, res_hbm, gain_hbm, w_hbm, out_hbm,
    qb, kb, vb, rate, res, gain, u, y, qf, before, lead,
    owned, fsend, frecv, esend, erecv, wbuf, abuf, pbuf,
    r1, r2, r3, p2, p3, p4,
    in_sem, w_send, w_recv, f_send, f_recv, e_send, e_recv,
    a_send, a_recv, x_send, x_recv, o_send, o_recv,
):
    ctx = lax.axis_index("ctx")
    ch = lax.axis_index("ch")
    z = lax.div(ctx, 4)
    q = lax.rem(ctx, 4)
    core = lax.rem(q, 2)
    y_hi = lax.div(q, 2)
    x = lax.div(ch, 2)
    y_lo = lax.rem(ch, 2)
    x0 = lax.rem(x, 2)
    x1 = lax.div(x, 2)
    near = lax.rem(x0 + x1, 2)
    far = x1
    near_ch = ch + 2 - 4 * x0
    far_ch = (3 - x) * 2 + y_lo
    y_ch = ch + 1 - 2 * y_lo
    sibling = ctx + 1 - 2 * core
    across = ctx + 2 - 4 * y_hi
    up = lax.rem(ctx + 4, CTX)
    down = lax.rem(ctx + CTX - 4, CTX)

    def block_at(j):
        return lax.rem(z + OFFSETS[j] + 8, 8)

    loads = []
    for place, (src, dst) in enumerate(
        ((k_hbm, kb), (v_hbm, vb), (rate_hbm, rate), (res_hbm, res), (gain_hbm, gain), (q_hbm, qb))
    ):
        loads.append(pltpu.make_async_copy(src, dst, in_sem.at[place]))
        loads[-1].start()
    w_own = pltpu.make_async_copy(w_hbm, wbuf.at[q], in_sem.at[6])
    w_own.start()

    bar = pltpu.get_barrier_semaphore()

    def greet(c, h):
        pl.semaphore_signal(bar, inc=1, device_id=(c, h), device_id_type=MESH)

    def greet_ctx(k, carry):
        greet(lax.rem(ctx + k, CTX), ch)
        return carry

    lax.fori_loop(1, CTX, greet_ctx, 0)
    for h in (near_ch, far_ch, y_ch):
        greet(ctx, h)
    is_home = ch == z

    def greet_ends(i, carry):
        @pl.when(jnp.logical_not(jnp.logical_and(is_home, i == z)))
        def _():
            greet(i * 4 + q, z)
            greet(ch * 4 + q, i)

        return carry

    lax.fori_loop(0, 8, greet_ends, 0)
    pl.semaphore_wait(bar, jnp.where(is_home, 34 + 14, 34 + 16))

    def w_copy(src, slot, place, target):
        return pltpu.make_async_remote_copy(
            src_ref=src, dst_ref=wbuf.at[slot], send_sem=w_send.at[place], recv_sem=w_recv.at[place],
            device_id=(target, ch), device_id_type=MESH,
        )

    w_across = w_copy(w_hbm, q, 0, across)
    w_across.start()
    w_sibling = w_copy(w_hbm, q, 1, sibling)
    w_sibling.start()

    for place in (0, 1, 2):
        loads[place].wait()
    chunk = lax.broadcasted_iota(jnp.int32, (POLES, CHUNKS, 128), 1)

    def lanes_of(g):
        return pl.ds(pl.multiple_of(g * 128, 128), 128)

    def tokens_at(p):
        return pl.ds(p, CHUNKS, stride=STEPS)

    def ending(g, carry):
        lanes = lanes_of(g)
        u[g] = kb[:, lanes].astype(F32) * vb[:, lanes].astype(F32)
        rows = rate[:, lanes]
        decay = spread(jnp.exp(-rows))
        state = jnp.zeros((POLES, CHUNKS, 128), F32)
        for p in range(STEPS):
            state = state * decay + u[g, tokens_at(p), :][None]
        for reach in (1, 2, 4):
            over = spread(jnp.exp(-rows * (STEPS * reach)))
            moved = pltpu.roll(state, reach, 1)
            state = state + jnp.where(chunk >= reach, over * moved, 0.0)
        before[g] = jnp.where(chunk >= 1, pltpu.roll(state, 1, 1), 0.0)
        owned[pl.ds(lax.div(g, 4) * POLES, POLES), lax.rem(g, 4), :] = rows
        fsend[pl.ds(lax.div(g, 4) * POLES, POLES), lax.rem(g, 4), :] = state[:, CHUNKS - 1, :]
        return carry

    lax.fori_loop(0, 8, ending, 0)

    def f_copy(k):
        owner = lax.rem(ctx + k, CTX)
        return pltpu.make_async_remote_copy(
            src_ref=fsend.at[owner], dst_ref=frecv.at[ctx], send_sem=f_send, recv_sem=f_recv,
            device_id=(owner, ch), device_id_type=MESH,
        )

    def f_start(k, carry):
        f_copy(k).start()
        return carry

    lax.fori_loop(1, CTX, f_start, 0)
    frecv[ctx] = fsend[ctx]

    for place in (3, 4, 5):
        loads[place].wait()

    def inside(g, carry):
        lanes = lanes_of(g)
        rows = rate[:, lanes]
        coef_rows = res[:, lanes] * jnp.sqrt(one_minus_exp(2.0 * rows))
        decay = spread(jnp.exp(-rows))
        coef = spread(coef_rows)
        lead[g] = coef * jnp.exp(-spread(rows) * (1.0 + STEPS * chunk.astype(F32)))
        direct = jnp.broadcast_to(gain[0:1, lanes], (CHUNKS, 128))
        qf[g] = qb[:, lanes].astype(F32)
        state = before[g]
        for p in range(STEPS):
            token = u[g, tokens_at(p), :]
            state = state * decay + token[None]
            y[g, tokens_at(p), :] = direct * token + jnp.sum(coef * state, axis=0)
        return carry

    lax.fori_loop(0, 4, inside, 0)

    bulk = pl.ds(0, CTX - 1)
    pltpu.make_async_copy(frecv.at[bulk], frecv.at[bulk], f_recv).wait()
    pltpu.make_async_copy(fsend.at[bulk], fsend.at[bulk], f_send).wait()
    own_decay = jnp.exp(-owned[ctx] * ROWS)
    entry = jnp.zeros((4, 128), F32)
    for i in range(CTX):
        esend[i] = entry
        entry = entry * own_decay + frecv[i]

    def e_start(k, carry):
        target = lax.rem(ctx + k, CTX)
        pltpu.make_async_remote_copy(
            src_ref=esend.at[target], dst_ref=erecv.at[ctx], send_sem=e_send, recv_sem=e_recv,
            device_id=(target, ch), device_id_type=MESH,
        ).start()
        return carry

    lax.fori_loop(1, CTX, e_start, 0)
    erecv[ctx] = esend[ctx]
    lax.fori_loop(4, 8, inside, 0)

    w_across.wait_recv()
    across_slot = lax.rem(q + 2, 4)
    w_onward = w_copy(wbuf.at[across_slot], across_slot, 2, sibling)
    w_onward.start()

    pltpu.make_async_copy(erecv.at[bulk], erecv.at[bulk], e_recv).wait()
    pltpu.make_async_copy(esend.at[bulk], esend.at[bulk], e_send).wait()

    def a_copy(r, way, c):
        src = 0 if r == 1 else 2 * (r - 1) - 1 + way
        dst = 7 if r == 4 else 2 * r - 1 + way
        place = ((r - 1) * 2 + way) * 2 + c
        return pltpu.make_async_remote_copy(
            src_ref=abuf.at[src, c], dst_ref=abuf.at[dst, c],
            send_sem=a_send.at[place], recv_sem=a_recv.at[place],
            device_id=((up, down)[way], ch), device_id_type=MESH,
        )

    def finish(c):
        def one(g, carry):
            lanes = lanes_of(g)
            decay = spread(jnp.exp(-rate[:, lanes]))
            rest = lead[g] * spread(erecv[pl.ds(lax.div(g, 4) * POLES, POLES), lax.rem(g, 4), :])
            for p in range(STEPS):
                y[g, tokens_at(p), :] = qf[g, tokens_at(p), :] * (
                    y[g, tokens_at(p), :] + jnp.sum(rest, axis=0)
                )
                rest = rest * decay
            abuf[0, c, :, lanes_of(lax.rem(g, 4))] = y[g].astype(BF)
            return carry

        lax.fori_loop(4 * c, 4 * c + 4, one, 0)

    a_copies = {}

    def a_go(r, way, c):
        a_copies[r, way, c] = a_copy(r, way, c)
        a_copies[r, way, c].start()

    for c in range(2):
        finish(c)
        for way in range(2):
            a_go(1, way, c)

    def a_arrive(r, c):
        for way in range(2):
            if r < 4 or way == c:
                a_copies[r, way, c].wait_recv()
                if r < 3 or (r == 3 and way == c):
                    a_go(r + 1, way, c)

    def product(slots):
        count = len(slots)

        def one(s, carry):
            for h in range(2):
                total = None
                for c in range(2):
                    left = jnp.concatenate([abuf[j, c] for j in slots], axis=0) if count > 1 else abuf[slots[0], c]
                    term = jnp.dot(
                        left, wbuf[2 * s + h, c * 512 : (c + 1) * 512, :], preferred_element_type=F32
                    )
                    total = term if total is None else total + term
                total = total.astype(BF)
                for n, j in enumerate(slots):
                    pbuf[j, s, :, h * 256 : (h + 1) * 256] = total[n * ROWS : (n + 1) * ROWS]
            return carry

        lax.fori_loop(0, 2, one, 0)

    first_bit = (near, far)
    second_bit = (far, near)
    first_ch = (near_ch, far_ch)
    second_ch = (far_ch, near_ch)

    def rows_at(bit, size):
        return pl.ds(pl.multiple_of(bit * size, size), size)

    x_copies = {}

    def x_go(stage, j, s):
        if stage == 1:
            src, dst, target = pbuf.at[j, s, rows_at(1 - first_bit[s], 64)], r1.at[j, s], first_ch[s]
        elif stage == 2:
            src, dst, target = p2.at[j, s, rows_at(1 - second_bit[s], 32)], r2.at[j, s], second_ch[s]
        else:
            src, dst, target = p3.at[j, s, rows_at(1 - y_lo, 16)], r3.at[j, s], y_ch
        place = ((stage - 1) * 8 + j) * 2 + s
        x_copies[stage, j, s] = pltpu.make_async_remote_copy(
            src_ref=src, dst_ref=dst, send_sem=x_send.at[place], recv_sem=x_recv.at[place],
            device_id=(ctx, target), device_id_type=MESH,
        )
        x_copies[stage, j, s].start()

    def x_take(stage, j, s):
        x_copies[stage, j, s].wait_recv()
        if stage == 1:
            mine, came, dst = pbuf[j, s, rows_at(first_bit[s], 64), :], r1[j, s], p2
        elif stage == 2:
            mine, came, dst = p2[j, s, rows_at(second_bit[s], 32), :], r2[j, s], p3
        else:
            mine, came, dst = p3[j, s, rows_at(y_lo, 16), :], r3[j, s], p4
        dst[j, s] = (mine.astype(F32) + came.astype(F32)).astype(BF)

    def step(stage, slots):
        for j in slots:
            for s in range(2):
                if stage:
                    x_take(stage, j, s)
                if stage < 3:
                    x_go(stage + 1, j, s)
                else:
                    place_out(j, s)

    def out_copy(j, s, local):
        rows = first_bit[s] * 64 + second_bit[s] * 32 + y_lo * 16
        dst = out_hbm.at[pl.ds(pl.multiple_of(rows, 16), 16), pl.ds(s * 512, 512)]
        if local:
            return pltpu.make_async_copy(p4.at[j, s], dst, o_recv)
        return pltpu.make_async_remote_copy(
            src_ref=p4.at[j, s], dst_ref=dst, send_sem=o_send, recv_sem=o_recv,
            device_id=(block_at(j) * 4 + q, z), device_id_type=MESH,
        )

    def place_out(j, s):
        if j:
            out_copy(j, s, False).start()
        else:
            @pl.when(is_home)
            def _():
                out_copy(j, s, True).start()

            @pl.when(jnp.logical_not(is_home))
            def _():
                out_copy(j, s, False).start()

    w_own.wait()
    w_sibling.wait_recv()
    w_onward.wait_recv()
    product(ROUNDS[0])
    step(0, ROUNDS[0])
    for r in (1, 2, 3, 4):
        a_arrive(r, 0)
        step(1, ROUNDS[r - 1])
        a_arrive(r, 1)
        product(ROUNDS[r])
        step(0, ROUNDS[r])
        step(2, ROUNDS[r - 1])
        if r >= 2:
            step(3, ROUNDS[r - 2])
    step(1, ROUNDS[4])
    step(3, ROUNDS[3])
    step(2, ROUNDS[4])
    step(3, ROUNDS[4])

    w_across.wait_send()
    w_sibling.wait_send()
    w_onward.wait_send()
    for copy in a_copies.values():
        copy.wait_send()
    for copy in x_copies.values():
        copy.wait_send()
    for j in range(8):
        for s in range(2):
            if j:
                out_copy(j, s, False).wait_send()
            else:
                @pl.when(jnp.logical_not(is_home))
                def _():
                    out_copy(j, s, False).wait_send()
    pltpu.make_async_copy(out_hbm, out_hbm, o_recv).wait()


def shards(query_proj, key_proj, value_proj, pole_rate, residue, direct_gain, out_weight):
    vmem = pltpu.VMEM
    dma = pltpu.SemaphoreType.DMA
    block = (ROWS, WIDTH)
    grouped = (8, ROWS, 128)
    tables = (8, POLES, CHUNKS, 128)
    return pl.pallas_call(
        kernel,
        out_shape=jax.ShapeDtypeStruct(block, BF),
        in_specs=[pl.BlockSpec(memory_space=pl.ANY)] * 7,
        out_specs=pl.BlockSpec(memory_space=pl.ANY),
        scratch_shapes=[
            vmem(block, BF), vmem(block, BF), vmem(block, BF),
            vmem((POLES, WIDTH), F32), vmem((POLES, WIDTH), F32), vmem((1, WIDTH), F32),
            vmem(grouped, F32), vmem(grouped, F32), vmem(grouped, F32),
            vmem(tables, F32), vmem(tables, F32),
            vmem((CTX, 4, 128), F32),
            vmem((CTX, 4, 128), F32), vmem((CTX, 4, 128), F32),
            vmem((CTX, 4, 128), F32), vmem((CTX, 4, 128), F32),
            vmem((4, WIDTH, 256), BF), vmem((8, 2, ROWS, 512), BF), vmem((8, 2, ROWS, 512), BF),
            vmem((8, 2, 64, 512), BF), vmem((8, 2, 32, 512), BF), vmem((8, 2, 16, 512), BF),
            vmem((8, 2, 64, 512), BF), vmem((8, 2, 32, 512), BF), vmem((8, 2, 16, 512), BF),
            dma((7,)), dma((3,)), dma((3,)), dma, dma, dma, dma,
            dma((16,)), dma((16,)), dma((48,)), dma((48,)), dma, dma,
        ],
        compiler_params=pltpu.CompilerParams(
            collective_id=0, has_side_effects=True, vmem_limit_bytes=40 * 1024 * 1024
        ),
        cost_estimate=pl.CostEstimate(flops=2**31, bytes_accessed=2**21, transcendentals=2**18),
    )(
        query_proj, key_proj, value_proj, pole_rate, residue,
        direct_gain.reshape(1, WIDTH), out_weight,
    )


def solution(mesh):
    return jax.shard_map(
        shards,
        mesh=mesh,
        in_specs=(
            P("ctx", "ch"),
            P("ctx", "ch"),
            P("ctx", "ch"),
            P(None, "ch"),
            P(None, "ch"),
            P("ch"),
            P("ch", "ctx"),
        ),
        out_specs=P("ctx", "ch"),
        check_vma=False,
    )
```

time: 395 us -> 84.4 us (0.21)
  waiting for transfers between devices: 359 us -> 0 us
  Pallas kernels: 0 us -> 77.1 us
  between operations: 13.7 us -> 0.02 us
  matrix products: 9.47 us -> 0 us
  other arithmetic: 6.89 us -> 0 us
    all_gather x3 -> x0, waiting for transfers between devices: 307 us -> none  [the longest x2 158 us: entering(): gathered = jax.tree.map(lambda a: lax.all_gather(a, axis), part)]
    pallas_call x0 -> x1, Pallas kernels: none -> 77.1 us  [shards(): pl.pallas_call(kernel, out_shape=jax.ShapeDtypeStruct(block, BF), in_spec...]
    reduce_scatter x1 -> x0, waiting for transfers between devices: 50.3 us -> none  [shards(): lax.psum_scatter(terms.astype(jnp.bfloat16), 'ch', scatter_dimension=1, t...]
    dot_general x1 -> x0, matrix products: 9.47 us -> none  [shards(): jnp.dot(hidden, lax.all_gather(out_weight, 'ctx', axis=1, tiled=True), pr...]
    unnamed x43 -> x15, local copies, waits for them, and re-layouts: 0.45 us -> 6.96 us
  transfers between devices with their start and end apart: 4 -> 0, of which waited for: 4 -> 0; matrix products, arithmetic and copies ran while one was open for 1% -> 0% of each run, Pallas kernels for 0% -> 0%
where the time goes in v1:
time: 84.4 us; the launch traced here: 84.1 us
  Pallas kernels  77.1 us (91%)
  local copies, waits for them, and re-layouts  6.96 us (8%)
    pallas_call x1, Pallas kernels, shards(): pl.pallas_call(kernel, out_shape=jax.ShapeDtypeStruct(block, BF), in_spec...  77.1 us
    unnamed x15, local copies, waits for them, and re-layouts  6.96 us

profile of v1, /device:TPU:4, one launch (start us, length us, event | category | flops | bytes accessed | tf_op | source)
XLA Modules:
  0.0 84.1 jit_solution(1675809215720954925)
XLA Ops:
  0.0 0.0 copy-start
  0.0 1.0 %copy-done = bf16[1024,256]{1,0:T(8,128)(2,1)S(1)} copy-done((bf16[1024,256]{1,0:T(8,128)(2,1)S(1)}, bf16[1024,256]{1,0:T(8,128)(2,1)}, u32[]{:S(2)}) %copy-start) | copy-done | bytes 524312
  1.0 0.0 copy-start.1
  1.0 0.9 %copy-done.1 = bf16[128,1024]{1,0:T(8,128)(2,1)S(1)} copy-done((bf16[128,1024]{1,0:T(8,128)(2,1)S(1)}, bf16[128,1024]{1,0:T(8,128)(2,1)}, u32[]{:S(2)}) %copy-start.1) | copy-done | bytes 262168
  2.0 0.0 copy-start.2
  2.0 0.9 %copy-done.2 = bf16[128,1024]{1,0:T(8,128)(2,1)S(1)} copy-done((bf16[128,1024]{1,0:T(8,128)(2,1)S(1)}, bf16[128,1024]{1,0:T(8,128)(2,1)}, u32[]{:S(2)}) %copy-start.2) | copy-done | bytes 262168
  2.9 0.0 copy-start.3
  2.9 0.9 %copy-done.3 = bf16[128,1024]{1,0:T(8,128)(2,1)S(1)} copy-done((bf16[128,1024]{1,0:T(8,128)(2,1)S(1)}, bf16[128,1024]{1,0:T(8,128)(2,1)}, u32[]{:S(2)}) %copy-start.3) | copy-done | bytes 262168
  3.9 0.0 copy-start.4
  3.9 0.8 copy-done.4
  4.7 0.0 copy-start.5
  4.7 0.8 copy-done.5
  5.6 0.0 copy-start.6
  5.6 0.7 copy-done.6
  6.3 77.1 %shard_map.73 = bf16[128,1024]{1,0:T(8,128)(2,1)S(1)} custom-call(bf16[128,1024]{1,0:T(8,128)(2,1)S(1)} %copy-done.1, bf16[128,1024]{1,0:T(8,128)(2,1)S(1)} %copy-done.2, bf16[128,1024]{1,0:T(8,128)(2,1)S(1)} %copy-done.3, f32[16,1024]{1,0:T(8,128)S(1)} %copy-done.4, f32[16,1024]{1,0:T(8,128)S(1)} %copy-done.5, f32[1,1024]{1,0:T(1,128)S(1)} %bitcast.1, ...), custom_call_target="tpu_custom_call" | custom-call | flops 2147483648 | bytes 2097152 | tf_op jit(solution)/shard_map/pallas_call | solution.py:372
  83.4 0.7 copy.9
Async XLA Ops:
  0.0 1.0 %copy-start = (bf16[1024,256]{1,0:T(8,128)(2,1)S(1)}, bf16[1024,256]{1,0:T(8,128)(2,1)}, u32[]{:S(2)}) copy-start(bf16[1024,256]{1,0:T(8,128)(2,1)} %w_hbm.1) | copy-start | bytes 1572868
  1.0 0.9 %copy-start.1 = (bf16[128,1024]{1,0:T(8,128)(2,1)S(1)}, bf16[128,1024]{1,0:T(8,128)(2,1)}, u32[]{:S(2)}) copy-start(bf16[128,1024]{1,0:T(8,128)(2,1)} %q_hbm.1) | copy-start | bytes 786436
  2.0 0.9 %copy-start.2 = (bf16[128,1024]{1,0:T(8,128)(2,1)S(1)}, bf16[128,1024]{1,0:T(8,128)(2,1)}, u32[]{:S(2)}) copy-start(bf16[128,1024]{1,0:T(8,128)(2,1)} %k_hbm.1) | copy-start | bytes 786436
  2.9 0.9 %copy-start.3 = (bf16[128,1024]{1,0:T(8,128)(2,1)S(1)}, bf16[128,1024]{1,0:T(8,128)(2,1)}, u32[]{:S(2)}) copy-start(bf16[128,1024]{1,0:T(8,128)(2,1)} %v_hbm.1) | copy-start | bytes 786436
  3.9 0.8 copy-start.4
  4.7 0.8 copy-start.5
  5.6 0.7 copy-start.6

commit v2 on v1

v2 whole, which is shorter than its diff:
```python
import jax
import jax.numpy as jnp
from jax import lax
from jax.experimental import pallas as pl
from jax.experimental.pallas import tpu as pltpu
from jax.sharding import PartitionSpec as P

MESH = pl.DeviceIdType.MESH
BF = jnp.bfloat16
F32 = jnp.float32
POLES = 16
ROWS = 128
WIDTH = 1024
CHUNKS = 8
STEPS = 16
CTX = 32
PARTS = 4
AROUND = ((2, 1), (2, 0), (1, 1), (3, 1), (1, 0), (3, 0), (0, 1))
OFFSETS = (0, -1, 1, -2, 2, -3, 3, 4)
ROUNDS = ((0,), (1, 2), (3, 4), (5, 6), (7,))


def one_minus_exp(x):
    series = 1.0 - x / 8.0
    for k in (7.0, 6.0, 5.0, 4.0, 3.0, 2.0):
        series = 1.0 - x / k * series
    return jnp.where(x < 0.125, x * series, 1.0 - jnp.exp(-x))


def spread(rows):
    return jnp.broadcast_to(rows[:, None, :], (POLES, CHUNKS, 128))


def kernel(
    q_hbm, k_hbm, v_hbm, rate_hbm, res_hbm, gain_hbm, w_hbm, out_hbm,
    qb, kb, vb, rate, res, gain, u, y, qf, before, lead,
    owned, fsend, frecv, esend, erecv, wbuf, abuf, pbuf,
    rbuf, sums,
    in_sem, w_send, w_recv, f_send, f_recv, e_send, e_recv,
    a_send, a_recv, x_send, x_recv, o_send, o_recv,
):
    ctx = lax.axis_index("ctx")
    ch = lax.axis_index("ch")
    z = lax.div(ctx, 4)
    q = lax.rem(ctx, 4)
    core = lax.rem(q, 2)
    y_hi = lax.div(q, 2)
    x = lax.div(ch, 2)
    y_lo = lax.rem(ch, 2)
    sibling = ctx + 1 - 2 * core
    across = ctx + 2 - 4 * y_hi
    up = lax.rem(ctx + 4, CTX)
    down = lax.rem(ctx + CTX - 4, CTX)

    def block_at(j):
        return lax.rem(z + OFFSETS[j] + 8, 8)

    loads = []
    for place, (src, dst) in enumerate(
        ((k_hbm, kb), (v_hbm, vb), (rate_hbm, rate), (res_hbm, res), (gain_hbm, gain), (q_hbm, qb))
    ):
        loads.append(pltpu.make_async_copy(src, dst, in_sem.at[place]))
        loads[-1].start()
    w_own = pltpu.make_async_copy(w_hbm, wbuf.at[q], in_sem.at[6])
    w_own.start()

    bar = pltpu.get_barrier_semaphore()

    def greet(c, h):
        pl.semaphore_signal(bar, inc=1, device_id=(c, h), device_id_type=MESH)

    def greet_ctx(k, carry):
        greet(lax.rem(ctx + k, CTX), ch)
        return carry

    lax.fori_loop(1, CTX, greet_ctx, 0)
    def greet_ch(k, carry):
        greet(ctx, lax.rem(ch + k, 8))
        return carry

    lax.fori_loop(1, 8, greet_ch, 0)
    is_home = ch == z

    def greet_ends(i, carry):
        @pl.when(jnp.logical_not(jnp.logical_and(is_home, i == z)))
        def _():
            greet(i * 4 + q, z)
            greet(ch * 4 + q, i)

        return carry

    lax.fori_loop(0, 8, greet_ends, 0)
    pl.semaphore_wait(bar, jnp.where(is_home, 38 + 14, 38 + 16))

    for place in (0, 1, 2):
        loads[place].wait()
    chunk = lax.broadcasted_iota(jnp.int32, (POLES, CHUNKS, 128), 1)

    def lanes_of(g):
        return pl.ds(pl.multiple_of(g * 128, 128), 128)

    def tokens_at(p):
        return pl.ds(p, CHUNKS, stride=STEPS)

    def ending(g, carry):
        lanes = lanes_of(g)
        u[g] = kb[:, lanes].astype(F32) * vb[:, lanes].astype(F32)
        rows = rate[:, lanes]
        decay = spread(jnp.exp(-rows))
        state = jnp.zeros((POLES, CHUNKS, 128), F32)
        for p in range(STEPS):
            state = state * decay + u[g, tokens_at(p), :][None]
        for reach in (1, 2, 4):
            over = spread(jnp.exp(-rows * (STEPS * reach)))
            moved = pltpu.roll(state, reach, 1)
            state = state + jnp.where(chunk >= reach, over * moved, 0.0)
        before[g] = jnp.where(chunk >= 1, pltpu.roll(state, 1, 1), 0.0)
        owned[pl.ds(lax.div(g, 4) * POLES, POLES), lax.rem(g, 4), :] = rows
        fsend[pl.ds(lax.div(g, 4) * POLES, POLES), lax.rem(g, 4), :] = state[:, CHUNKS - 1, :]
        return carry

    lax.fori_loop(0, 8, ending, 0)

    def peer(k):
        t = lax.div(lax.rem(k, 16), 2)
        dz = 4 + lax.div(t + 1, 2) * (1 - 2 * lax.rem(t, 2))
        dy = 1 - lax.div(k, 16)
        dc = 1 - lax.rem(k, 2)
        return lax.rem(z + dz, 8) * 4 + lax.rem(y_hi + dy, 2) * 2 + lax.rem(core + dc, 2)

    def f_start(k, carry):
        owner = peer(k)
        pltpu.make_async_remote_copy(
            src_ref=fsend.at[owner], dst_ref=frecv.at[ctx], send_sem=f_send, recv_sem=f_recv,
            device_id=(owner, ch), device_id_type=MESH,
        ).start()
        return carry

    lax.fori_loop(0, CTX - 1, f_start, 0)

    def w_copy(src, slot, part, place, target):
        rows = pl.ds(part * 512, 512)
        return pltpu.make_async_remote_copy(
            src_ref=src.at[rows], dst_ref=wbuf.at[slot, rows],
            send_sem=w_send.at[place, part], recv_sem=w_recv.at[place, part],
            device_id=(target, ch), device_id_type=MESH,
        )

    w_across = [w_copy(w_hbm, q, part, 0, across) for part in range(2)]
    w_sibling = [w_copy(w_hbm, q, part, 1, sibling) for part in range(2)]
    w_across[0].start()
    frecv[ctx] = fsend[ctx]

    for place in (3, 4, 5):
        loads[place].wait()

    def inside(g, carry):
        lanes = lanes_of(g)
        rows = rate[:, lanes]
        coef_rows = res[:, lanes] * jnp.sqrt(one_minus_exp(2.0 * rows))
        decay = spread(jnp.exp(-rows))
        coef = spread(coef_rows)
        lead[g] = coef * jnp.exp(-spread(rows) * (1.0 + STEPS * chunk.astype(F32)))
        direct = jnp.broadcast_to(gain[0:1, lanes], (CHUNKS, 128))
        qf[g] = qb[:, lanes].astype(F32)
        state = before[g]
        for p in range(STEPS):
            token = u[g, tokens_at(p), :]
            state = state * decay + token[None]
            y[g, tokens_at(p), :] = direct * token + jnp.sum(coef * state, axis=0)
        return carry

    lax.fori_loop(0, 4, inside, 0)

    bulk = pl.ds(0, CTX - 1)
    pltpu.make_async_copy(frecv.at[bulk], frecv.at[bulk], f_recv).wait()
    pltpu.make_async_copy(fsend.at[bulk], fsend.at[bulk], f_send).wait()
    own_decay = jnp.exp(-owned[ctx] * ROWS)
    entry = jnp.zeros((4, 128), F32)
    for i in range(CTX):
        esend[i] = entry
        entry = entry * own_decay + frecv[i]

    def e_start(k, carry):
        target = peer(k)
        pltpu.make_async_remote_copy(
            src_ref=esend.at[target], dst_ref=erecv.at[ctx], send_sem=e_send, recv_sem=e_recv,
            device_id=(target, ch), device_id_type=MESH,
        ).start()
        return carry

    lax.fori_loop(0, CTX - 1, e_start, 0)
    w_across[1].start()
    for copy in w_sibling:
        copy.start()
    erecv[ctx] = esend[ctx]
    lax.fori_loop(4, 8, inside, 0)

    across_slot = lax.rem(q + 2, 4)
    w_onward = [w_copy(wbuf.at[across_slot], across_slot, part, 2, sibling) for part in range(2)]
    w_across[0].wait_recv()
    w_onward[0].start()

    pltpu.make_async_copy(erecv.at[bulk], erecv.at[bulk], e_recv).wait()
    pltpu.make_async_copy(esend.at[bulk], esend.at[bulk], e_send).wait()

    def a_copy(r, way, c):
        src = 0 if r == 1 else 2 * (r - 1) - 1 + way
        dst = 7 if r == 4 else 2 * r - 1 + way
        place = ((r - 1) * 2 + way) * PARTS + c
        return pltpu.make_async_remote_copy(
            src_ref=abuf.at[src, c], dst_ref=abuf.at[dst, c],
            send_sem=a_send.at[place], recv_sem=a_recv.at[place],
            device_id=((up, down)[way], ch), device_id_type=MESH,
        )

    def last_way(c):
        return c // (PARTS // 2)

    def finish(g, carry):
        lanes = lanes_of(g)
        decay = spread(jnp.exp(-rate[:, lanes]))
        rest = lead[g] * spread(erecv[pl.ds(lax.div(g, 4) * POLES, POLES), lax.rem(g, 4), :])
        for p in range(STEPS):
            y[g, tokens_at(p), :] = qf[g, tokens_at(p), :] * (
                y[g, tokens_at(p), :] + jnp.sum(rest, axis=0)
            )
            rest = rest * decay
        abuf[0, lax.div(g, 2), :, lanes_of(lax.rem(g, 2))] = y[g].astype(BF)
        return carry

    a_copies = {}

    def a_go(r, way, c):
        a_copies[r, way, c] = a_copy(r, way, c)
        a_copies[r, way, c].start()

    for c in range(PARTS):
        lax.fori_loop(2 * c, 2 * c + 2, finish, 0)
        for way in range(2):
            a_go(1, way, c)

    def a_arrive(r):
        for c in range(PARTS):
            for way in range(2):
                if r < 4 or way == last_way(c):
                    a_copies[r, way, c].wait_recv()
                    if r < 3 or (r == 3 and way == last_way(c)):
                        a_go(r + 1, way, c)

    def product(slots):
        def one(n, carry):
            total = None
            for c in range(PARTS):
                left = jnp.concatenate([abuf[j, c] for j in slots], axis=0) if len(slots) > 1 else abuf[slots[0], c]
                term = jnp.dot(
                    left, wbuf[n, c * 256 : (c + 1) * 256, :], preferred_element_type=F32
                )
                total = term if total is None else total + term
            total = total.astype(BF)
            columns = pl.ds(pl.multiple_of(n * 256, 256), 256)
            for place, j in enumerate(slots):
                pbuf[j, :, columns] = total[place * ROWS : (place + 1) * ROWS]
            return carry

        lax.fori_loop(0, 4, one, 0)

    def piece(owner):
        return pl.ds(pl.multiple_of(owner * 16, 16), 16)

    x_copies = []

    def scatter(slots):
        for j in slots:
            for place, (dx, dy) in enumerate(AROUND):
                owner = lax.rem(x + dx, 4) * 2 + lax.rem(y_lo + dy, 2)
                x_copies.append(
                    pltpu.make_async_remote_copy(
                        src_ref=pbuf.at[j, piece(owner)], dst_ref=rbuf.at[j, place],
                        send_sem=x_send, recv_sem=x_recv.at[j],
                        device_id=(ctx, owner), device_id_type=MESH,
                    )
                )
                x_copies[-1].start()

    def out_copy(j, local):
        dst = out_hbm.at[piece(ch)]
        if local:
            return pltpu.make_async_copy(sums.at[j], dst, o_recv)
        return pltpu.make_async_remote_copy(
            src_ref=sums.at[j], dst_ref=dst, send_sem=o_send, recv_sem=o_recv,
            device_id=(block_at(j) * 4 + q, z), device_id_type=MESH,
        )

    def gather(slots):
        for j in slots:
            pltpu.make_async_copy(rbuf.at[j], rbuf.at[j], x_recv.at[j]).wait()
            total = pbuf[j, piece(ch), :].astype(F32)
            for place in range(len(AROUND)):
                total = total + rbuf[j, place].astype(F32)
            sums[j] = total.astype(BF)
            if j:
                out_copy(j, False).start()
            else:
                @pl.when(is_home)
                def _():
                    out_copy(j, True).start()

                @pl.when(jnp.logical_not(is_home))
                def _():
                    out_copy(j, False).start()

    w_own.wait()
    w_across[1].wait_recv()
    w_onward[1].start()
    for part in range(2):
        w_sibling[part].wait_recv()
        w_onward[part].wait_recv()
    product(ROUNDS[0])
    scatter(ROUNDS[0])
    for r in (1, 2, 3, 4):
        a_arrive(r)
        product(ROUNDS[r])
        scatter(ROUNDS[r])
        if r >= 2:
            gather(ROUNDS[r - 2])
    gather(ROUNDS[3])
    gather(ROUNDS[4])

    for copy in (*w_across, *w_sibling, *w_onward, *a_copies.values()):
        copy.wait_send()
    pltpu.make_async_copy(rbuf, rbuf, x_send).wait()
    later = sums.at[pl.ds(1, 7)]
    pltpu.make_async_copy(later, later, o_send).wait()

    @pl.when(jnp.logical_not(is_home))
    def _():
        pltpu.make_async_copy(sums.at[0], sums.at[0], o_send).wait()

    pltpu.make_async_copy(out_hbm, out_hbm, o_recv).wait()


def shards(query_proj, key_proj, value_proj, pole_rate, residue, direct_gain, out_weight):
    vmem = pltpu.VMEM
    dma = pltpu.SemaphoreType.DMA
    block = (ROWS, WIDTH)
    grouped = (8, ROWS, 128)
    tables = (8, POLES, CHUNKS, 128)
    return pl.pallas_call(
        kernel,
        out_shape=jax.ShapeDtypeStruct(block, BF),
        in_specs=[pl.BlockSpec(memory_space=pltpu.HBM)] * 7,
        out_specs=pl.BlockSpec(memory_space=pltpu.HBM),
        scratch_shapes=[
            vmem(block, BF), vmem(block, BF), vmem(block, BF),
            vmem((POLES, WIDTH), F32), vmem((POLES, WIDTH), F32), vmem((1, WIDTH), F32),
            vmem(grouped, F32), vmem(grouped, F32), vmem(grouped, F32),
            vmem(tables, F32), vmem(tables, F32),
            vmem((CTX, 4, 128), F32),
            vmem((CTX, 4, 128), F32), vmem((CTX, 4, 128), F32),
            vmem((CTX, 4, 128), F32), vmem((CTX, 4, 128), F32),
            vmem((4, WIDTH, 256), BF), vmem((8, PARTS, ROWS, 256), BF), vmem((8, ROWS, WIDTH), BF),
            vmem((8, len(AROUND), 16, WIDTH), BF), vmem((8, 16, WIDTH), BF),
            dma((7,)), dma((3, 2)), dma((3, 2)), dma, dma, dma, dma,
            dma((8 * PARTS,)), dma((8 * PARTS,)), dma, dma((8,)), dma, dma,
        ],
        compiler_params=pltpu.CompilerParams(
            collective_id=0, has_side_effects=True, vmem_limit_bytes=48 * 1024 * 1024
        ),
        cost_estimate=pl.CostEstimate(flops=2**31, bytes_accessed=2**21, transcendentals=2**18),
    )(
        *(
            pltpu.with_memory_space_constraint(a, pltpu.HBM)
            for a in (
                query_proj, key_proj, value_proj, pole_rate, residue,
                direct_gain.reshape(1, WIDTH), out_weight,
            )
        )
    )


def solution(mesh):
    return jax.shard_map(
        shards,
        mesh=mesh,
        in_specs=(
            P("ctx", "ch"),
            P("ctx", "ch"),
            P("ctx", "ch"),
            P(None, "ch"),
            P(None, "ch"),
            P("ch"),
            P("ch", "ctx"),
        ),
        out_specs=P("ctx", "ch"),
        check_vma=False,
    )
```

time: 84.4 us -> 66.3 us (0.79)
  Pallas kernels: 77.1 us -> 65.5 us
  local copies, waits for them, and re-layouts: 6.96 us -> 0.71 us
    pallas_call x1, Pallas kernels: 77.1 us -> 65.5 us  [shards(): pl.pallas_call(kernel, out_shape=jax.ShapeDtypeStruct(block, BF), in_spec...]
    unnamed x15 -> x1, local copies, waits for them, and re-layouts: 6.96 us -> 0.71 us
where the time goes in v2:
time: 66.3 us
  Pallas kernels  65.5 us (99%)
  local copies, waits for them, and re-layouts  0.71 us (1%)
    pallas_call x1, Pallas kernels, shards(): pl.pallas_call(kernel, out_shape=jax.ShapeDtypeStruct(block, BF), in_spec...  65.5 us

profile of v2, /device:TPU:4, one launch (start us, length us, event | category | flops | bytes accessed | tf_op | source)
XLA Modules:
  0.0 66.3 jit_solution(1334165779171984264)
XLA Ops:
  0.0 65.5 %shard_map.73 = bf16[128,1024]{1,0:T(8,128)(2,1)S(1)} custom-call(bf16[128,1024]{1,0:T(8,128)(2,1)} %q_hbm.1, bf16[128,1024]{1,0:T(8,128)(2,1)} %k_hbm.1, bf16[128,1024]{1,0:T(8,128)(2,1)} %v_hbm.1, f32[16,1024]{1,0:T(8,128)} %rate_hbm.1, f32[16,1024]{1,0:T(8,128)} %res_hbm.1, f32[1,1024]{1,0:T(1,128)} %bitcast.1, bf16[1024,256]{1,0:T(8,128)(2,1)} %w_hbm.1), custom_call_target="tpu_custom_call" | custom-call | flops 2147483648 | bytes 2097152 | tf_op jit(solution)/shard_map/pallas_call | solution.py:349
  65.5 0.7 %copy.9 = bf16[128,1024]{1,0:T(8,128)(2,1)} copy(bf16[128,1024]{1,0:T(8,128)(2,1)S(1)} %shard_map.73) | data formatting | bytes 524288

commit v3 on v2

--- a/solution.py
+++ b/solution.py
@@ -34,9 +34,9 @@
 def kernel(
     q_hbm, k_hbm, v_hbm, rate_hbm, res_hbm, gain_hbm, w_hbm, out_hbm,
     qb, kb, vb, rate, res, gain, u, y, qf, before, lead,
-    owned, fsend, frecv, esend, erecv, wbuf, abuf, pbuf,
+    fsend, fgroup, dgroup, tsend, trecv, esend, entry, wbuf, abuf, pbuf,
     rbuf, sums,
-    in_sem, w_send, w_recv, f_send, f_recv, e_send, e_recv,
+    in_sem, w_send, w_recv, f_send, f_recv, t_send, t_recv, e_send, e_recv,
     a_send, a_recv, x_send, x_recv, o_send, o_recv,
 ):
     ctx = lax.axis_index("ctx")
@@ -49,6 +49,7 @@
     y_lo = lax.rem(ch, 2)
     sibling = ctx + 1 - 2 * core
     across = ctx + 2 - 4 * y_hi
+    beyond = z * 4 + 3 - q
     up = lax.rem(ctx + 4, CTX)
     down = lax.rem(ctx + CTX - 4, CTX)
 
@@ -69,11 +70,14 @@
     def greet(c, h):
         pl.semaphore_signal(bar, inc=1, device_id=(c, h), device_id_type=MESH)
 
-    def greet_ctx(k, carry):
-        greet(lax.rem(ctx + k, CTX), ch)
-        return carry
-
-    lax.fori_loop(1, CTX, greet_ctx, 0)
+    for c in (sibling, across, beyond):
+        greet(c, ch)
+
+    def greet_z(k, carry):
+        greet(lax.rem(ctx + 4 * k, CTX), ch)
+        return carry
+
+    lax.fori_loop(1, 8, greet_z, 0)
     def greet_ch(k, carry):
         greet(ctx, lax.rem(ch + k, 8))
         return carry
@@ -90,7 +94,7 @@
         return carry
 
     lax.fori_loop(0, 8, greet_ends, 0)
-    pl.semaphore_wait(bar, jnp.where(is_home, 38 + 14, 38 + 16))
+    pl.semaphore_wait(bar, jnp.where(is_home, 17 + 14, 17 + 16))
 
     for place in (0, 1, 2):
         loads[place].wait()
@@ -115,28 +119,20 @@
             moved = pltpu.roll(state, reach, 1)
             state = state + jnp.where(chunk >= reach, over * moved, 0.0)
         before[g] = jnp.where(chunk >= 1, pltpu.roll(state, 1, 1), 0.0)
-        owned[pl.ds(lax.div(g, 4) * POLES, POLES), lax.rem(g, 4), :] = rows
-        fsend[pl.ds(lax.div(g, 4) * POLES, POLES), lax.rem(g, 4), :] = state[:, CHUNKS - 1, :]
+        fsend[lax.div(g, 4), :, lanes_of(lax.rem(g, 4))] = state[:, CHUNKS - 1, :]
         return carry
 
     lax.fori_loop(0, 8, ending, 0)
 
-    def peer(k):
-        t = lax.div(lax.rem(k, 16), 2)
-        dz = 4 + lax.div(t + 1, 2) * (1 - 2 * lax.rem(t, 2))
-        dy = 1 - lax.div(k, 16)
-        dc = 1 - lax.rem(k, 2)
-        return lax.rem(z + dz, 8) * 4 + lax.rem(y_hi + dy, 2) * 2 + lax.rem(core + dc, 2)
-
-    def f_start(k, carry):
-        owner = peer(k)
+    f_copies = [
         pltpu.make_async_remote_copy(
-            src_ref=fsend.at[owner], dst_ref=frecv.at[ctx], send_sem=f_send, recv_sem=f_recv,
-            device_id=(owner, ch), device_id_type=MESH,
-        ).start()
-        return carry
-
-    lax.fori_loop(0, CTX - 1, f_start, 0)
+            src_ref=fsend.at[half], dst_ref=fgroup.at[q], send_sem=f_send.at[place], recv_sem=f_recv.at[place],
+            device_id=(target, ch), device_id_type=MESH,
+        )
+        for place, (half, target) in enumerate(((core, across), (1 - core, beyond), (1 - core, sibling)))
+    ]
+    for copy in f_copies:
+        copy.start()
 
     def w_copy(src, slot, part, place, target):
         rows = pl.ds(part * 512, 512)
@@ -148,8 +144,9 @@
 
     w_across = [w_copy(w_hbm, q, part, 0, across) for part in range(2)]
     w_sibling = [w_copy(w_hbm, q, part, 1, sibling) for part in range(2)]
-    w_across[0].start()
-    frecv[ctx] = fsend[ctx]
+    for copy in (*w_across, *w_sibling):
+        copy.start()
+    fgroup[q] = fsend[core]
 
     for place in (3, 4, 5):
         loads[place].wait()
@@ -172,37 +169,46 @@
 
     lax.fori_loop(0, 4, inside, 0)
 
-    bulk = pl.ds(0, CTX - 1)
-    pltpu.make_async_copy(frecv.at[bulk], frecv.at[bulk], f_recv).wait()
-    pltpu.make_async_copy(fsend.at[bulk], fsend.at[bulk], f_send).wait()
-    own_decay = jnp.exp(-owned[ctx] * ROWS)
-    entry = jnp.zeros((4, 128), F32)
-    for i in range(CTX):
-        esend[i] = entry
-        entry = entry * own_decay + frecv[i]
-
-    def e_start(k, carry):
-        target = peer(k)
-        pltpu.make_async_remote_copy(
-            src_ref=esend.at[target], dst_ref=erecv.at[ctx], send_sem=e_send, recv_sem=e_recv,
-            device_id=(target, ch), device_id_type=MESH,
-        ).start()
-        return carry
-
-    lax.fori_loop(0, CTX - 1, e_start, 0)
-    w_across[1].start()
-    for copy in w_sibling:
-        copy.start()
-    erecv[ctx] = esend[ctx]
+    for copy in f_copies:
+        copy.wait_recv()
+    half_rows = rate[:, pl.ds(pl.multiple_of(core * 512, 512), 512)]
+    own_decay = jnp.exp(-half_rows * ROWS)
+    group_decay = jnp.exp(-half_rows * (4 * ROWS))
+    total = jnp.zeros((POLES, 512), F32)
+    for i in range(4):
+        dgroup[i] = total
+        total = total * own_decay + fgroup[i]
+    tsend[...] = total.astype(BF)
+
+    def t_copy(dz):
+        return pltpu.make_async_remote_copy(
+            src_ref=tsend, dst_ref=trecv.at[z], send_sem=t_send.at[dz], recv_sem=t_recv.at[z],
+            device_id=(lax.rem(ctx + 4 * dz, CTX), ch), device_id_type=MESH,
+        )
+
+    for dz in (4, 3, 5, 2, 6, 1, 7):
+        @pl.when(z + dz < 8)
+        def _():
+            t_copy(dz).start()
+
     lax.fori_loop(4, 8, inside, 0)
 
-    across_slot = lax.rem(q + 2, 4)
-    w_onward = [w_copy(wbuf.at[across_slot], across_slot, part, 2, sibling) for part in range(2)]
-    w_across[0].wait_recv()
-    w_onward[0].start()
-
-    pltpu.make_async_copy(erecv.at[bulk], erecv.at[bulk], e_recv).wait()
-    pltpu.make_async_copy(esend.at[bulk], esend.at[bulk], e_send).wait()
+    def earlier(i, so_far):
+        pltpu.make_async_copy(trecv.at[i], trecv.at[i], t_recv.at[i]).wait()
+        return so_far * group_decay + trecv[i].astype(F32)
+
+    so_far = lax.fori_loop(0, z, earlier, jnp.zeros((POLES, 512), F32))
+
+    def entry_of(place):
+        return so_far * jnp.exp(-half_rows * (ROWS * place).astype(F32)) + dgroup[place]
+
+    esend[...] = entry_of(q + 1 - 2 * core)
+    e_copy = pltpu.make_async_remote_copy(
+        src_ref=esend, dst_ref=entry.at[core], send_sem=e_send, recv_sem=e_recv,
+        device_id=(sibling, ch), device_id_type=MESH,
+    )
+    e_copy.start()
+    entry[core] = entry_of(q)
 
     def a_copy(r, way, c):
         src = 0 if r == 1 else 2 * (r - 1) - 1 + way
@@ -214,19 +220,17 @@
             device_id=((up, down)[way], ch), device_id_type=MESH,
         )
 
-    def last_way(c):
-        return c // (PARTS // 2)
-
-    def finish(g, carry):
+    def finish(k, carry):
+        g = lax.rem(4 * core + k, 8)
         lanes = lanes_of(g)
         decay = spread(jnp.exp(-rate[:, lanes]))
-        rest = lead[g] * spread(erecv[pl.ds(lax.div(g, 4) * POLES, POLES), lax.rem(g, 4), :])
+        rest = lead[g] * spread(entry[lax.div(g, 4), :, lanes_of(lax.rem(g, 4))])
         for p in range(STEPS):
             y[g, tokens_at(p), :] = qf[g, tokens_at(p), :] * (
                 y[g, tokens_at(p), :] + jnp.sum(rest, axis=0)
             )
             rest = rest * decay
-        abuf[0, lax.div(g, 2), :, lanes_of(lax.rem(g, 2))] = y[g].astype(BF)
+        abuf[0, lax.div(k, 2), :, lanes_of(lax.rem(k, 2))] = y[g].astype(BF)
         return carry
 
     a_copies = {}
@@ -235,17 +239,21 @@
         a_copies[r, way, c] = a_copy(r, way, c)
         a_copies[r, way, c].start()
 
+    order = tuple(zip((0, 2, 1, 3), (1, 3, 0, 2)))
     for c in range(PARTS):
+        if c == 2:
+            e_copy.wait_recv()
         lax.fori_loop(2 * c, 2 * c + 2, finish, 0)
-        for way in range(2):
-            a_go(1, way, c)
+        a_go(1, c % 2, c)
+    for way, c in ((0, 1), (1, 0), (0, 3), (1, 2)):
+        a_go(1, way, c)
 
     def a_arrive(r):
-        for c in range(PARTS):
-            for way in range(2):
-                if r < 4 or way == last_way(c):
+        for pair in order:
+            for way, c in enumerate(pair):
+                if r < 4 or way == c % 2:
                     a_copies[r, way, c].wait_recv()
-                    if r < 3 or (r == 3 and way == last_way(c)):
+                    if r < 3 or (r == 3 and way == c % 2):
                         a_go(r + 1, way, c)
 
     def product(slots):
@@ -253,9 +261,8 @@
             total = None
             for c in range(PARTS):
                 left = jnp.concatenate([abuf[j, c] for j in slots], axis=0) if len(slots) > 1 else abuf[slots[0], c]
-                term = jnp.dot(
-                    left, wbuf[n, c * 256 : (c + 1) * 256, :], preferred_element_type=F32
-                )
+                rows = pl.ds(pl.multiple_of(lax.rem(2 * core + c, PARTS) * 256, 256), 256)
+                term = jnp.dot(left, wbuf[n, rows, :], preferred_element_type=F32)
                 total = term if total is None else total + term
             total = total.astype(BF)
             columns = pl.ds(pl.multiple_of(n * 256, 256), 256)
@@ -311,8 +318,11 @@
                     out_copy(j, False).start()
 
     w_own.wait()
-    w_across[1].wait_recv()
-    w_onward[1].start()
+    across_slot = lax.rem(q + 2, 4)
+    w_onward = [w_copy(wbuf.at[across_slot], across_slot, part, 2, sibling) for part in range(2)]
+    for part in range(2):
+        w_across[part].wait_recv()
+        w_onward[part].start()
     for part in range(2):
         w_sibling[part].wait_recv()
         w_onward[part].wait_recv()
@@ -327,8 +337,13 @@
     gather(ROUNDS[3])
     gather(ROUNDS[4])
 
-    for copy in (*w_across, *w_sibling, *w_onward, *a_copies.values()):
+    for copy in (*f_copies, *w_across, *w_sibling, e_copy, *w_onward, *a_copies.values()):
         copy.wait_send()
+    for dz in range(1, 8):
+        @pl.when(z + dz < 8)
+        def _():
+            t_copy(dz).wait_send()
+
     pltpu.make_async_copy(rbuf, rbuf, x_send).wait()
     later = sums.at[pl.ds(1, 7)]
     pltpu.make_async_copy(later, later, o_send).wait()
@@ -356,12 +371,12 @@
             vmem((POLES, WIDTH), F32), vmem((POLES, WIDTH), F32), vmem((1, WIDTH), F32),
             vmem(grouped, F32), vmem(grouped, F32), vmem(grouped, F32),
             vmem(tables, F32), vmem(tables, F32),
-            vmem((CTX, 4, 128), F32),
-            vmem((CTX, 4, 128), F32), vmem((CTX, 4, 128), F32),
-            vmem((CTX, 4, 128), F32), vmem((CTX, 4, 128), F32),
+            vmem((2, POLES, 512), F32), vmem((4, POLES, 512), F32), vmem((4, POLES, 512), F32),
+            vmem((POLES, 512), BF), vmem((8, POLES, 512), BF),
+            vmem((POLES, 512), F32), vmem((2, POLES, 512), F32),
             vmem((4, WIDTH, 256), BF), vmem((8, PARTS, ROWS, 256), BF), vmem((8, ROWS, WIDTH), BF),
             vmem((8, len(AROUND), 16, WIDTH), BF), vmem((8, 16, WIDTH), BF),
-            dma((7,)), dma((3, 2)), dma((3, 2)), dma, dma, dma, dma,
+            dma((7,)), dma((3, 2)), dma((3, 2)), dma((3,)), dma((3,)), dma((8,)), dma((8,)), dma, dma,
             dma((8 * PARTS,)), dma((8 * PARTS,)), dma, dma((8,)), dma, dma,
         ],
         compiler_params=pltpu.CompilerParams(

time: 66.3 us -> 64.5 us (0.973)
  Pallas kernels: 65.5 us -> 63.7 us
    pallas_call x1, Pallas kernels: 65.5 us -> 63.7 us  [shards(): pl.pallas_call(kernel, out_shape=jax.ShapeDtypeStruct(block, BF), in_spec...]
where the time goes in v3:
time: 64.5 us; the launch traced here: 64.4 us
  Pallas kernels  63.7 us (99%)
  local copies, waits for them, and re-layouts  0.71 us (1%)
    pallas_call x1, Pallas kernels, shards(): pl.pallas_call(kernel, out_shape=jax.ShapeDtypeStruct(block, BF), in_spec...  63.7 us

profile of v3, /device:TPU:4, one launch (start us, length us, event | category | flops | bytes accessed | tf_op | source)
XLA Modules:
  0.0 64.4 jit_solution(1640944253030989050)
XLA Ops:
  0.0 63.7 %shard_map.73 = bf16[128,1024]{1,0:T(8,128)(2,1)S(1)} custom-call(bf16[128,1024]{1,0:T(8,128)(2,1)} %q_hbm.1, bf16[128,1024]{1,0:T(8,128)(2,1)} %k_hbm.1, bf16[128,1024]{1,0:T(8,128)(2,1)} %v_hbm.1, f32[16,1024]{1,0:T(8,128)} %rate_hbm.1, f32[16,1024]{1,0:T(8,128)} %res_hbm.1, f32[1,1024]{1,0:T(1,128)} %bitcast.1, bf16[1024,256]{1,0:T(8,128)(2,1)} %w_hbm.1), custom_call_target="tpu_custom_call" | custom-call | flops 2147483648 | bytes 2097152 | tf_op jit(solution)/shard_map/pallas_call | solution.py:364
  63.7 0.7 %copy.9 = bf16[128,1024]{1,0:T(8,128)(2,1)} copy(bf16[128,1024]{1,0:T(8,128)(2,1)S(1)} %shard_map.73) | data formatting | bytes 524288

commit v4 on v3

--- a/solution.py
+++ b/solution.py
@@ -85,16 +85,7 @@
     lax.fori_loop(1, 8, greet_ch, 0)
     is_home = ch == z
 
-    def greet_ends(i, carry):
-        @pl.when(jnp.logical_not(jnp.logical_and(is_home, i == z)))
-        def _():
-            greet(i * 4 + q, z)
-            greet(ch * 4 + q, i)
-
-        return carry
-
-    lax.fori_loop(0, 8, greet_ends, 0)
-    pl.semaphore_wait(bar, jnp.where(is_home, 17 + 14, 17 + 16))
+    pl.semaphore_wait(bar, 17)
 
     for place in (0, 1, 2):
         loads[place].wait()
@@ -167,7 +158,7 @@
             y[g, tokens_at(p), :] = direct * token + jnp.sum(coef * state, axis=0)
         return carry
 
-    lax.fori_loop(0, 4, inside, 0)
+    lax.fori_loop(0, 8, inside, 0)
 
     for copy in f_copies:
         copy.wait_recv()
@@ -190,8 +181,6 @@
         @pl.when(z + dz < 8)
         def _():
             t_copy(dz).start()
-
-    lax.fori_loop(4, 8, inside, 0)
 
     def earlier(i, so_far):
         pltpu.make_async_copy(trecv.at[i], trecv.at[i], t_recv.at[i]).wait()

time: 64.5 us -> 62.6 us (0.971)
  Pallas kernels: 63.7 us -> 61.7 us
    pallas_call x1, Pallas kernels: 63.7 us -> 61.7 us  [shards(): pl.pallas_call(kernel, out_shape=jax.ShapeDtypeStruct(block, BF), in_spec...]
where the time goes in v4:
time: 62.6 us; the launch traced here: 62.4 us
  Pallas kernels  61.7 us (99%)
  local copies, waits for them, and re-layouts  0.71 us (1%)
    pallas_call x1, Pallas kernels, shards(): pl.pallas_call(kernel, out_shape=jax.ShapeDtypeStruct(block, BF), in_spec...  61.7 us

profile of v4, /device:TPU:4, one launch (start us, length us, event | category | flops | bytes accessed | tf_op | source)
XLA Modules:
  0.0 62.4 jit_solution(3888553976173635013)
XLA Ops:
  0.0 61.7 %shard_map.73 = bf16[128,1024]{1,0:T(8,128)(2,1)S(1)} custom-call(bf16[128,1024]{1,0:T(8,128)(2,1)} %q_hbm.1, bf16[128,1024]{1,0:T(8,128)(2,1)} %k_hbm.1, bf16[128,1024]{1,0:T(8,128)(2,1)} %v_hbm.1, f32[16,1024]{1,0:T(8,128)} %rate_hbm.1, f32[16,1024]{1,0:T(8,128)} %res_hbm.1, f32[1,1024]{1,0:T(1,128)} %bitcast.1, bf16[1024,256]{1,0:T(8,128)(2,1)} %w_hbm.1), custom_call_target="tpu_custom_call" | custom-call | flops 2147483648 | bytes 2097152 | tf_op jit(solution)/shard_map/pallas_call | solution.py:353
  61.7 0.7 %copy.9 = bf16[128,1024]{1,0:T(8,128)(2,1)} copy(bf16[128,1024]{1,0:T(8,128)(2,1)S(1)} %shard_map.73) | data formatting | bytes 524288

commit v5 on v4

--- a/solution.py
+++ b/solution.py
@@ -14,10 +14,9 @@
 CHUNKS = 8
 STEPS = 16
 CTX = 32
-PARTS = 4
+PARTS = 2
 AROUND = ((2, 1), (2, 0), (1, 1), (3, 1), (1, 0), (3, 0), (0, 1))
-OFFSETS = (0, -1, 1, -2, 2, -3, 3, 4)
-ROUNDS = ((0,), (1, 2), (3, 4), (5, 6), (7,))
+STAGED = 7
 
 
 def one_minus_exp(x):
@@ -34,8 +33,8 @@
 def kernel(
     q_hbm, k_hbm, v_hbm, rate_hbm, res_hbm, gain_hbm, w_hbm, out_hbm,
     qb, kb, vb, rate, res, gain, u, y, qf, before, lead,
-    fsend, fgroup, dgroup, tsend, trecv, esend, entry, wbuf, abuf, pbuf,
-    rbuf, sums,
+    fsend, fgroup, dgroup, tsend, trecv, esend, entry, wbuf, abuf,
+    part, r1, p2, r2, r7, sums,
     in_sem, w_send, w_recv, f_send, f_recv, t_send, t_recv, e_send, e_recv,
     a_send, a_recv, x_send, x_recv, o_send, o_recv,
 ):
@@ -47,14 +46,17 @@
     y_hi = lax.div(q, 2)
     x = lax.div(ch, 2)
     y_lo = lax.rem(ch, 2)
+    x0 = lax.rem(x, 2)
+    x1 = lax.div(x, 2)
+    near = lax.rem(x0 + x1, 2)
+    far = x1
+    near_ch = ch + 2 - 4 * x0
+    far_ch = (3 - x) * 2 + y_lo
     sibling = ctx + 1 - 2 * core
     across = ctx + 2 - 4 * y_hi
     beyond = z * 4 + 3 - q
     up = lax.rem(ctx + 4, CTX)
     down = lax.rem(ctx + CTX - 4, CTX)
-
-    def block_at(j):
-        return lax.rem(z + OFFSETS[j] + 8, 8)
 
     loads = []
     for place, (src, dst) in enumerate(
@@ -84,7 +86,6 @@
 
     lax.fori_loop(1, 8, greet_ch, 0)
     is_home = ch == z
-
     pl.semaphore_wait(bar, 17)
 
     for place in (0, 1, 2):
@@ -93,6 +94,9 @@
 
     def lanes_of(g):
         return pl.ds(pl.multiple_of(g * 128, 128), 128)
+
+    def half_of(c):
+        return pl.ds(pl.multiple_of(c * 512, 512), 512)
 
     def tokens_at(p):
         return pl.ds(p, CHUNKS, stride=STEPS)
@@ -162,7 +166,7 @@
 
     for copy in f_copies:
         copy.wait_recv()
-    half_rows = rate[:, pl.ds(pl.multiple_of(core * 512, 512), 512)]
+    half_rows = rate[:, half_of(core)]
     own_decay = jnp.exp(-half_rows * ROWS)
     group_decay = jnp.exp(-half_rows * (4 * ROWS))
     total = jnp.zeros((POLES, 512), F32)
@@ -204,7 +208,7 @@
         dst = 7 if r == 4 else 2 * r - 1 + way
         place = ((r - 1) * 2 + way) * PARTS + c
         return pltpu.make_async_remote_copy(
-            src_ref=abuf.at[src, c], dst_ref=abuf.at[dst, c],
+            src_ref=abuf.at[src, pl.ds(c * 64, 64)], dst_ref=abuf.at[dst, pl.ds(c * 64, 64)],
             send_sem=a_send.at[place], recv_sem=a_recv.at[place],
             device_id=((up, down)[way], ch), device_id_type=MESH,
         )
@@ -219,7 +223,7 @@
                 y[g, tokens_at(p), :] + jnp.sum(rest, axis=0)
             )
             rest = rest * decay
-        abuf[0, lax.div(k, 2), :, lanes_of(lax.rem(k, 2))] = y[g].astype(BF)
+        abuf[0, :, lanes] = y[g].astype(BF)
         return carry
 
     a_copies = {}
@@ -228,103 +232,184 @@
         a_copies[r, way, c] = a_copy(r, way, c)
         a_copies[r, way, c].start()
 
-    order = tuple(zip((0, 2, 1, 3), (1, 3, 0, 2)))
-    for c in range(PARTS):
-        if c == 2:
-            e_copy.wait_recv()
-        lax.fori_loop(2 * c, 2 * c + 2, finish, 0)
-        a_go(1, c % 2, c)
-    for way, c in ((0, 1), (1, 0), (0, 3), (1, 2)):
+    lax.fori_loop(0, 4, finish, 0)
+    e_copy.wait_recv()
+    lax.fori_loop(4, 8, finish, 0)
+    for way, c in ((0, 0), (1, 1), (0, 1), (1, 0)):
         a_go(1, way, c)
 
-    def a_arrive(r):
-        for pair in order:
-            for way, c in enumerate(pair):
-                if r < 4 or way == c % 2:
-                    a_copies[r, way, c].wait_recv()
-                    if r < 3 or (r == 3 and way == c % 2):
-                        a_go(r + 1, way, c)
-
-    def product(slots):
-        def one(n, carry):
-            total = None
-            for c in range(PARTS):
-                left = jnp.concatenate([abuf[j, c] for j in slots], axis=0) if len(slots) > 1 else abuf[slots[0], c]
-                rows = pl.ds(pl.multiple_of(lax.rem(2 * core + c, PARTS) * 256, 256), 256)
-                term = jnp.dot(left, wbuf[n, rows, :], preferred_element_type=F32)
-                total = term if total is None else total + term
-            total = total.astype(BF)
-            columns = pl.ds(pl.multiple_of(n * 256, 256), 256)
-            for place, j in enumerate(slots):
-                pbuf[j, :, columns] = total[place * ROWS : (place + 1) * ROWS]
+    def a_arrive(r, i):
+        for way in range(2):
+            c = (way + i) % 2
+            a_copies[r, way, c].wait_recv()
+            if r < 3 or (r == 3 and i == 0):
+                a_go(r + 1, way, c)
+
+    def product(left, side, store):
+        def one(h, carry):
+            total = jnp.dot(left(), wbuf[2 * side + h], preferred_element_type=F32)
+            store(pl.ds(pl.multiple_of(h * 256, 256), 256), total.astype(BF))
             return carry
 
-        lax.fori_loop(0, 4, one, 0)
-
-    def piece(owner):
-        return pl.ds(pl.multiple_of(owner * 16, 16), 16)
-
-    x_copies = []
-
-    def scatter(slots):
-        for j in slots:
-            for place, (dx, dy) in enumerate(AROUND):
-                owner = lax.rem(x + dx, 4) * 2 + lax.rem(y_lo + dy, 2)
-                x_copies.append(
-                    pltpu.make_async_remote_copy(
-                        src_ref=pbuf.at[j, piece(owner)], dst_ref=rbuf.at[j, place],
-                        send_sem=x_send, recv_sem=x_recv.at[j],
-                        device_id=(ctx, owner), device_id_type=MESH,
-                    )
-                )
-                x_copies[-1].start()
-
-    def out_copy(j, local):
-        dst = out_hbm.at[piece(ch)]
-        if local:
-            return pltpu.make_async_copy(sums.at[j], dst, o_recv)
-        return pltpu.make_async_remote_copy(
-            src_ref=sums.at[j], dst_ref=dst, send_sem=o_send, recv_sem=o_recv,
-            device_id=(block_at(j) * 4 + q, z), device_id_type=MESH,
-        )
-
-    def gather(slots):
-        for j in slots:
-            pltpu.make_async_copy(rbuf.at[j], rbuf.at[j], x_recv.at[j]).wait()
-            total = pbuf[j, piece(ch), :].astype(F32)
-            for place in range(len(AROUND)):
-                total = total + rbuf[j, place].astype(F32)
-            sums[j] = total.astype(BF)
-            if j:
-                out_copy(j, False).start()
-            else:
-                @pl.when(is_home)
-                def _():
-                    out_copy(j, True).start()
-
-                @pl.when(jnp.logical_not(is_home))
-                def _():
-                    out_copy(j, False).start()
-
-    w_own.wait()
+        lax.fori_loop(0, 2, one, 0)
+
+    def rows_at(start, size):
+        return pl.ds(pl.multiple_of(start, size), size)
+
+    def first_bit(s):
+        return near + s * (far - near)
+
+    def second_bit(s):
+        return far + s * (near - far)
+
+    def first_ch(s):
+        return near_ch + s * (far_ch - near_ch)
+
+    def second_ch(s):
+        return far_ch + s * (near_ch - far_ch)
+
+    def runs_of(t):
+        if t in (0, 7):
+            return ((t, 0), (t, 64))
+        r, second = (t + 1) // 2, (t + 1) % 2
+        return ((2 * r - 1, 64 * second), (2 * r, 64 - 64 * second))
+
+    def place_of(t, run):
+        if t in (0, 7):
+            return t // 7 * 4, 64 * run
+        r, second = (t + 1) // 2, (t + 1) % 2
+        return r * (2 * run - 1), (64 - 64 * run if second else 64 * run)
+
+    def multiply(t, s):
+        def left():
+            return jnp.concatenate([abuf[j, row : row + 64] for j, row in runs_of(t)], axis=0)
+
+        def store(columns, total):
+            for run in range(2):
+                part[t, run, s, :, columns] = total[run * 64 : (run + 1) * 64]
+
+        product(left, s, store)
+
+    def halves(t, s):
+        multiply(t, s)
+        pltpu.make_async_remote_copy(
+            src_ref=part.at[t, 1 - first_bit(s), s], dst_ref=r1.at[t, s],
+            send_sem=x_send.at[0], recv_sem=x_recv.at[t, s],
+            device_id=(ctx, first_ch(s)), device_id_type=MESH,
+        ).start()
+
+    def quarters(t):
+        for s in range(2):
+            pltpu.make_async_copy(r1.at[t, s], r1.at[t, s], x_recv.at[t, s]).wait()
+            p2[t, s] = (part[t, first_bit(s), s].astype(F32) + r1[t, s].astype(F32)).astype(BF)
+            for place, (turn, y_turn) in enumerate(((1, 1), (1, 0), (0, 1))):
+                bit = 1 - second_bit(s) if turn else second_bit(s)
+                y_bit = 1 - y_lo if y_turn else y_lo
+                target = second_ch(s) if turn else ch
+                pltpu.make_async_remote_copy(
+                    src_ref=p2.at[t, s, rows_at(bit * 32 + y_bit * 16, 16)], dst_ref=r2.at[t, s, place],
+                    send_sem=x_send.at[1], recv_sem=x_recv.at[8 + t, s],
+                    device_id=(ctx, target - y_lo + y_bit), device_id_type=MESH,
+                ).start()
+
+    def whole(t):
+        for s in range(2):
+            pltpu.make_async_copy(r2.at[t, s], r2.at[t, s], x_recv.at[8 + t, s]).wait()
+            row = second_bit(s) * 32 + y_lo * 16
+            total = p2[t, s, rows_at(row, 16), :].astype(F32)
+            for place in range(3):
+                total = total + r2[t, s, place].astype(F32)
+            sums[t, s] = total.astype(BF)
+            steps, start = place_of(t, first_bit(s))
+            place_out(sums.at[t, s], steps, start + row, s, t == 0)
+
+    def direct(t):
+        multiply(t, 0)
+        multiply(t, 1)
+        for place, (dx, dy) in enumerate(AROUND):
+            owner_x, owner_y = lax.rem(x + dx, 4), lax.rem(y_lo + dy, 2)
+            pltpu.make_async_remote_copy(
+                src_ref=part.at[t, :, owner_y, rows_at(owner_x * 16, 16)], dst_ref=r7.at[t - STAGED, place],
+                send_sem=x_send.at[2], recv_sem=x_recv.at[8 + t, 0],
+                device_id=(ctx, owner_x * 2 + owner_y), device_id_type=MESH,
+            ).start()
+
+    def direct_whole(t):
+        came = r7.at[t - STAGED]
+        pltpu.make_async_copy(came, came, x_recv.at[8 + t, 0]).wait()
+        total = part[t, :, y_lo, rows_at(x * 16, 16), :].astype(F32)
+        for place in range(len(AROUND)):
+            total = total + r7[t - STAGED, place].astype(F32)
+        sums[t] = total.astype(BF)
+        for run in range(2):
+            steps, start = place_of(t, run)
+            place_out(sums.at[t, run], steps, start + x * 16, y_lo)
+
+    def place_out(src, steps, row, s, own=False):
+        dst = out_hbm.at[rows_at(row, 16), half_of(s)]
+        block = lax.rem(z + steps + 8, 8)
+        remote = pltpu.make_async_remote_copy(
+            src_ref=src, dst_ref=dst, send_sem=o_send, recv_sem=o_recv,
+            device_id=(block * 4 + q, z), device_id_type=MESH,
+        )
+        if own:
+            @pl.when(is_home)
+            def _():
+                pltpu.make_async_copy(src, dst, o_recv).start()
+
+            @pl.when(jnp.logical_not(is_home))
+            def _():
+                remote.start()
+        else:
+            remote.start()
+
     across_slot = lax.rem(q + 2, 4)
     w_onward = [w_copy(wbuf.at[across_slot], across_slot, part, 2, sibling) for part in range(2)]
-    for part in range(2):
-        w_across[part].wait_recv()
-        w_onward[part].start()
-    for part in range(2):
-        w_sibling[part].wait_recv()
-        w_onward[part].wait_recv()
-    product(ROUNDS[0])
-    scatter(ROUNDS[0])
-    for r in (1, 2, 3, 4):
-        a_arrive(r)
-        product(ROUNDS[r])
-        scatter(ROUNDS[r])
-        if r >= 2:
-            gather(ROUNDS[r - 2])
-    gather(ROUNDS[3])
-    gather(ROUNDS[4])
+    w_own.wait()
+    for n in range(2):
+        w_sibling[n].wait_recv()
+    halves(0, y_hi)
+    for n in range(2):
+        w_across[n].wait_recv()
+        w_onward[n].start()
+    for n in range(2):
+        w_onward[n].wait_recv()
+    halves(0, 1 - y_hi)
+    a_arrive(1, 0)
+    halves(1, 0)
+    halves(1, 1)
+    a_arrive(1, 1)
+    halves(2, 0)
+    halves(2, 1)
+    quarters(0)
+    a_arrive(2, 0)
+    halves(3, 0)
+    halves(3, 1)
+    quarters(1)
+    a_arrive(2, 1)
+    halves(4, 0)
+    halves(4, 1)
+    quarters(2)
+    whole(0)
+    a_arrive(3, 0)
+    halves(5, 0)
+    halves(5, 1)
+    quarters(3)
+    whole(1)
+    a_arrive(3, 1)
+    halves(6, 0)
+    halves(6, 1)
+    quarters(4)
+    whole(2)
+    quarters(5)
+    a_arrive(4, 0)
+    direct(7)
+    whole(3)
+    quarters(6)
+    whole(4)
+    whole(5)
+    direct_whole(7)
+    whole(6)
 
     for copy in (*f_copies, *w_across, *w_sibling, e_copy, *w_onward, *a_copies.values()):
         copy.wait_send()
@@ -333,7 +418,9 @@
         def _():
             t_copy(dz).wait_send()
 
-    pltpu.make_async_copy(rbuf, rbuf, x_send).wait()
+    pltpu.make_async_copy(r1, r1, x_send.at[0]).wait()
+    pltpu.make_async_copy(r2, r2, x_send.at[1]).wait()
+    pltpu.make_async_copy(r7, r7, x_send.at[2]).wait()
     later = sums.at[pl.ds(1, 7)]
     pltpu.make_async_copy(later, later, o_send).wait()
 
@@ -363,10 +450,11 @@
             vmem((2, POLES, 512), F32), vmem((4, POLES, 512), F32), vmem((4, POLES, 512), F32),
             vmem((POLES, 512), BF), vmem((8, POLES, 512), BF),
             vmem((POLES, 512), F32), vmem((2, POLES, 512), F32),
-            vmem((4, WIDTH, 256), BF), vmem((8, PARTS, ROWS, 256), BF), vmem((8, ROWS, WIDTH), BF),
-            vmem((8, len(AROUND), 16, WIDTH), BF), vmem((8, 16, WIDTH), BF),
+            vmem((4, WIDTH, 256), BF), vmem((8, ROWS, WIDTH), BF), vmem((8, 2, 2, 64, 512), BF),
+            vmem((STAGED, 2, 64, 512), BF), vmem((STAGED, 2, 64, 512), BF), vmem((STAGED, 2, 3, 16, 512), BF),
+            vmem((8 - STAGED, len(AROUND), 2, 16, 512), BF), vmem((8, 2, 16, 512), BF),
             dma((7,)), dma((3, 2)), dma((3, 2)), dma((3,)), dma((3,)), dma((8,)), dma((8,)), dma, dma,
-            dma((8 * PARTS,)), dma((8 * PARTS,)), dma, dma((8,)), dma, dma,
+            dma((8 * PARTS,)), dma((8 * PARTS,)), dma((3,)), dma((16, 2)), dma, dma,
         ],
         compiler_params=pltpu.CompilerParams(
             collective_id=0, has_side_effects=True, vmem_limit_bytes=48 * 1024 * 1024

time: 62.6 us -> 62.1 us (level)
  no operation moved by 1% of the time
where the time goes in v5:
time: 62.1 us; the launch traced here: 62 us
  Pallas kernels  61.3 us (99%)
  local copies, waits for them, and re-layouts  0.71 us (1%)
    pallas_call x1, Pallas kernels, shards(): pl.pallas_call(kernel, out_shape=jax.ShapeDtypeStruct(block, BF), in_spec...  61.3 us

profile of v5, /device:TPU:4, one launch (start us, length us, event | category | flops | bytes accessed | tf_op | source)
XLA Modules:
  0.0 62.0 jit_solution(15210132245469949238)
XLA Ops:
  0.0 61.3 %shard_map.73 = bf16[128,1024]{1,0:T(8,128)(2,1)S(1)} custom-call(bf16[128,1024]{1,0:T(8,128)(2,1)} %q_hbm.1, bf16[128,1024]{1,0:T(8,128)(2,1)} %k_hbm.1, bf16[128,1024]{1,0:T(8,128)(2,1)} %v_hbm.1, f32[16,1024]{1,0:T(8,128)} %rate_hbm.1, f32[16,1024]{1,0:T(8,128)} %res_hbm.1, f32[1,1024]{1,0:T(1,128)} %bitcast.1, bf16[1024,256]{1,0:T(8,128)(2,1)} %w_hbm.1), custom_call_target="tpu_custom_call" | custom-call | flops 2147483648 | bytes 2097152 | tf_op jit(solution)/shard_map/pallas_call | solution.py:440
  61.3 0.7 %copy.9 = bf16[128,1024]{1,0:T(8,128)(2,1)} copy(bf16[128,1024]{1,0:T(8,128)(2,1)S(1)} %shard_map.73) | data formatting | bytes 524288

commit v6 on v5

--- a/solution.py
+++ b/solution.py
@@ -130,15 +130,15 @@
         copy.start()
 
     def w_copy(src, slot, part, place, target):
-        rows = pl.ds(part * 512, 512)
+        rows = pl.ds(part * 1024, 1024)
         return pltpu.make_async_remote_copy(
             src_ref=src.at[rows], dst_ref=wbuf.at[slot, rows],
             send_sem=w_send.at[place, part], recv_sem=w_recv.at[place, part],
             device_id=(target, ch), device_id_type=MESH,
         )
 
-    w_across = [w_copy(w_hbm, q, part, 0, across) for part in range(2)]
-    w_sibling = [w_copy(w_hbm, q, part, 1, sibling) for part in range(2)]
+    w_across = [w_copy(w_hbm, q, part, 0, across) for part in range(1)]
+    w_sibling = [w_copy(w_hbm, q, part, 1, sibling) for part in range(1)]
     for copy in (*w_across, *w_sibling):
         copy.start()
     fgroup[q] = fsend[core]
@@ -232,16 +232,31 @@
         a_copies[r, way, c] = a_copy(r, way, c)
         a_copies[r, way, c].start()
 
+    def a_first(way, h):
+        lanes = half_of(lax.rem(core + h, 2))
+        place = 8 * PARTS + 2 * way + h
+        return pltpu.make_async_remote_copy(
+            src_ref=abuf.at[0, pl.ds(way * 64, 64), lanes], dst_ref=abuf.at[1 + way, pl.ds(way * 64, 64), lanes],
+            send_sem=a_send.at[place], recv_sem=a_recv.at[place],
+            device_id=((up, down)[way], ch), device_id_type=MESH,
+        )
+
+    firsts = [[a_first(way, h) for h in range(2)] for way in range(2)]
     lax.fori_loop(0, 4, finish, 0)
+    for way in range(2):
+        firsts[way][0].start()
     e_copy.wait_recv()
     lax.fori_loop(4, 8, finish, 0)
-    for way, c in ((0, 0), (1, 1), (0, 1), (1, 0)):
-        a_go(1, way, c)
+    for way in range(2):
+        firsts[way][1].start()
+    for way in range(2):
+        a_go(1, way, 1 - way)
 
     def a_arrive(r, i):
         for way in range(2):
             c = (way + i) % 2
-            a_copies[r, way, c].wait_recv()
+            for copy in firsts[way] if r == 1 and i == 0 else (a_copies[r, way, c],):
+                copy.wait_recv()
             if r < 3 or (r == 3 and i == 0):
                 a_go(r + 1, way, c)
 
@@ -324,15 +339,17 @@
             place_out(sums.at[t, s], steps, start + row, s, t == 0)
 
     def direct(t):
-        multiply(t, 0)
-        multiply(t, 1)
-        for place, (dx, dy) in enumerate(AROUND):
-            owner_x, owner_y = lax.rem(x + dx, 4), lax.rem(y_lo + dy, 2)
-            pltpu.make_async_remote_copy(
-                src_ref=part.at[t, :, owner_y, rows_at(owner_x * 16, 16)], dst_ref=r7.at[t - STAGED, place],
-                send_sem=x_send.at[2], recv_sem=x_recv.at[8 + t, 0],
-                device_id=(ctx, owner_x * 2 + owner_y), device_id_type=MESH,
-            ).start()
+        for dy in (1, 0):
+            owner_y = lax.rem(y_lo + dy, 2)
+            multiply(t, owner_y)
+            for place, (dx, turn) in enumerate(AROUND):
+                if turn == dy:
+                    owner_x = lax.rem(x + dx, 4)
+                    pltpu.make_async_remote_copy(
+                        src_ref=part.at[t, :, owner_y, rows_at(owner_x * 16, 16)], dst_ref=r7.at[t - STAGED, place],
+                        send_sem=x_send.at[2], recv_sem=x_recv.at[8 + t, 0],
+                        device_id=(ctx, owner_x * 2 + owner_y), device_id_type=MESH,
+                    ).start()
 
     def direct_whole(t):
         came = r7.at[t - STAGED]
@@ -364,18 +381,18 @@
             remote.start()
 
     across_slot = lax.rem(q + 2, 4)
-    w_onward = [w_copy(wbuf.at[across_slot], across_slot, part, 2, sibling) for part in range(2)]
+    w_onward = [w_copy(wbuf.at[across_slot], across_slot, part, 2, sibling) for part in range(1)]
     w_own.wait()
-    for n in range(2):
+    for n in range(1):
         w_sibling[n].wait_recv()
     halves(0, y_hi)
-    for n in range(2):
+    for n in range(1):
         w_across[n].wait_recv()
         w_onward[n].start()
-    for n in range(2):
+    a_arrive(1, 0)
+    for n in range(1):
         w_onward[n].wait_recv()
     halves(0, 1 - y_hi)
-    a_arrive(1, 0)
     halves(1, 0)
     halves(1, 1)
     a_arrive(1, 1)
@@ -383,35 +400,35 @@
     halves(2, 1)
     quarters(0)
     a_arrive(2, 0)
+    quarters(1)
     halves(3, 0)
     halves(3, 1)
-    quarters(1)
     a_arrive(2, 1)
+    quarters(2)
     halves(4, 0)
     halves(4, 1)
-    quarters(2)
     whole(0)
     a_arrive(3, 0)
+    quarters(3)
     halves(5, 0)
     halves(5, 1)
-    quarters(3)
     whole(1)
     a_arrive(3, 1)
+    quarters(4)
     halves(6, 0)
     halves(6, 1)
-    quarters(4)
     whole(2)
     quarters(5)
     a_arrive(4, 0)
     direct(7)
+    quarters(6)
     whole(3)
-    quarters(6)
     whole(4)
     whole(5)
     direct_whole(7)
     whole(6)
 
-    for copy in (*f_copies, *w_across, *w_sibling, e_copy, *w_onward, *a_copies.values()):
+    for copy in (*f_copies, *w_across, *w_sibling, e_copy, *w_onward, *firsts[0], *firsts[1], *a_copies.values()):
         copy.wait_send()
     for dz in range(1, 8):
         @pl.when(z + dz < 8)
@@ -454,7 +471,7 @@
             vmem((STAGED, 2, 64, 512), BF), vmem((STAGED, 2, 64, 512), BF), vmem((STAGED, 2, 3, 16, 512), BF),
             vmem((8 - STAGED, len(AROUND), 2, 16, 512), BF), vmem((8, 2, 16, 512), BF),
             dma((7,)), dma((3, 2)), dma((3, 2)), dma((3,)), dma((3,)), dma((8,)), dma((8,)), dma, dma,
-            dma((8 * PARTS,)), dma((8 * PARTS,)), dma((3,)), dma((16, 2)), dma, dma,
+            dma((8 * PARTS + 4,)), dma((8 * PARTS + 4,)), dma((3,)), dma((16, 2)), dma, dma,
         ],
         compiler_params=pltpu.CompilerParams(
             collective_id=0, has_side_effects=True, vmem_limit_bytes=48 * 1024 * 1024

time: 62.1 us -> 59.7 us (0.961)
  Pallas kernels: 61.3 us -> 58.9 us
    pallas_call x1, Pallas kernels: 61.3 us -> 58.9 us  [shards(): pl.pallas_call(kernel, out_shape=jax.ShapeDtypeStruct(block, BF), in_spec...]
where the time goes in v6:
time: 59.7 us
  Pallas kernels  58.9 us (99%)
  local copies, waits for them, and re-layouts  0.71 us (1%)
    pallas_call x1, Pallas kernels, shards(): pl.pallas_call(kernel, out_shape=jax.ShapeDtypeStruct(block, BF), in_spec...  58.9 us

profile of v6, /device:TPU:4, one launch (start us, length us, event | category | flops | bytes accessed | tf_op | source)
XLA Modules:
  0.0 59.7 jit_solution(6692696501757620100)
XLA Ops:
  0.0 58.9 %shard_map.73 = bf16[128,1024]{1,0:T(8,128)(2,1)S(1)} custom-call(bf16[128,1024]{1,0:T(8,128)(2,1)} %q_hbm.1, bf16[128,1024]{1,0:T(8,128)(2,1)} %k_hbm.1, bf16[128,1024]{1,0:T(8,128)(2,1)} %v_hbm.1, f32[16,1024]{1,0:T(8,128)} %rate_hbm.1, f32[16,1024]{1,0:T(8,128)} %res_hbm.1, f32[1,1024]{1,0:T(1,128)} %bitcast.1, bf16[1024,256]{1,0:T(8,128)(2,1)} %w_hbm.1), custom_call_target="tpu_custom_call" | custom-call | flops 2147483648 | bytes 2097152 | tf_op jit(solution)/shard_map/pallas_call | solution.py:457
  58.9 0.7 %copy.9 = bf16[128,1024]{1,0:T(8,128)(2,1)} copy(bf16[128,1024]{1,0:T(8,128)(2,1)S(1)} %shard_map.73) | data formatting | bytes 524288

commit v7 on v6

--- a/solution.py
+++ b/solution.py
@@ -396,9 +396,9 @@
     halves(1, 0)
     halves(1, 1)
     a_arrive(1, 1)
+    quarters(0)
     halves(2, 0)
     halves(2, 1)
-    quarters(0)
     a_arrive(2, 0)
     quarters(1)
     halves(3, 0)

time: 59.7 us -> 61.3 us (1.027)
  Pallas kernels: 58.9 us -> 60.5 us
    pallas_call x1, Pallas kernels: 58.9 us -> 60.5 us  [shards(): pl.pallas_call(kernel, out_shape=jax.ShapeDtypeStruct(block, BF), in_spec...]
where the time goes in v7:
time: 61.3 us; the launch traced here: 61.2 us
  Pallas kernels  60.5 us (99%)
  local copies, waits for them, and re-layouts  0.71 us (1%)
    pallas_call x1, Pallas kernels, shards(): pl.pallas_call(kernel, out_shape=jax.ShapeDtypeStruct(block, BF), in_spec...  60.5 us

profile of v7, /device:TPU:4, one launch (start us, length us, event | category | flops | bytes accessed | tf_op | source)
XLA Modules:
  0.0 61.2 jit_solution(11166213513349480698)
XLA Ops:
  0.0 60.5 %shard_map.73 = bf16[128,1024]{1,0:T(8,128)(2,1)S(1)} custom-call(bf16[128,1024]{1,0:T(8,128)(2,1)} %q_hbm.1, bf16[128,1024]{1,0:T(8,128)(2,1)} %k_hbm.1, bf16[128,1024]{1,0:T(8,128)(2,1)} %v_hbm.1, f32[16,1024]{1,0:T(8,128)} %rate_hbm.1, f32[16,1024]{1,0:T(8,128)} %res_hbm.1, f32[1,1024]{1,0:T(1,128)} %bitcast.1, bf16[1024,256]{1,0:T(8,128)(2,1)} %w_hbm.1), custom_call_target="tpu_custom_call" | custom-call | flops 2147483648 | bytes 2097152 | tf_op jit(solution)/shard_map/pallas_call | solution.py:457
  60.5 0.7 %copy.9 = bf16[128,1024]{1,0:T(8,128)(2,1)} copy(bf16[128,1024]{1,0:T(8,128)(2,1)S(1)} %shard_map.73) | data formatting | bytes 524288
